TPU v7x, 32 devices: a whole 2x2x4 slice. The times are simulated.
32 devices in a mesh: groups: 2 (over y), shot: 8 (over z, x), ap: 2 (over core).
Axes of the slice: x: 2, y: 2, z: 4, core: 2. Of those that a mesh axis runs over, the one named last changes fastest.
Arguments:
- forward_field: bfloat16 [16, 16, 64, 128], P(('groups', 'shot'), 'ap'), parts along dimension 0, may hold values from -6 to 6
- forward_older: bfloat16 [16, 16, 64, 128], P(('groups', 'shot'), 'ap'), parts along dimension 0, may hold values from -6 to 6
- adjoint_field: bfloat16 [16, 16, 64, 128], P(('groups', 'shot'), 'ap'), parts along dimension 0, may hold values from -6 to 6
- adjoint_newer: bfloat16 [16, 16, 64, 128], P(('groups', 'shot'), 'ap'), parts along dimension 0, may hold values from -6 to 6
- velocity: float32 [32, 128, 192], P(('groups', 'ap'), 'shot'), parts along dimension 0, may hold values from 0.15 to 0.4
- anchor_first: int32 [16], P(('groups', 'shot')), parts along dimension 0, may hold values from 0 to 64
- anchor_second: int32 [16], P(('groups', 'shot')), parts along dimension 0, may hold values from 0 to 64
- wavelet: float32 [16, 4], P(('groups', 'shot')), parts along dimension 0, may hold values from -48 to 48
- source_cell: int32 [16], P(('groups', 'shot')), parts along dimension 0, may hold values from 0 to 131071
- receivers: int32 [16, 256], P(('groups', 'shot')), parts along dimension 0, may hold values from 0 to 131071
- traces: float32 [16, 4, 256], P(('groups', 'shot')), parts along dimension 0, may hold values from -24 to 24
Outputs:
- migrated_image: float32 [32, 128, 192], P(('groups', 'ap'), 'shot'), parts along dimension 0
There are 2 independent parts, one for each index of `groups`. A program takes and returns all parts, laid end to end along the dimension named above; each array names one. Nothing has to cross between parts.
All inputs are finite; a program needn't handle non-finite values.
Results may differ from a plain program's by a relative error of at most 0.0003.
Values may be sent and summed in bfloat16 or wider, within the bound.
A program may use at most 64 MiB of HBM per device.

v0:
```python
import jax
import jax.numpy as jnp
from jax import lax
from jax.sharding import PartitionSpec as P

STEPS = 4
GX = 128
GY = 192


STENCIL = (-205.0 / 72.0, 8.0 / 5.0, -1.0 / 5.0, 8.0 / 315.0, -1.0 / 560.0)


def with_halo(shard, sides, width):
    for axis, dim in sides:
        count, length = (lax.axis_size(axis), shard.shape[dim])
        up = [(i, (i + 1) % count) for i in range(count - 1)]
        down = [(j, i) for i, j in up]
        last = lax.slice_in_dim(shard, length - width, length, axis=dim)
        initial = lax.slice_in_dim(shard, 0, width, axis=dim)
        before = lax.ppermute(last, axis, up)
        after = lax.ppermute(initial, axis, down)
        shard = jnp.concatenate([before, shard, after], axis=dim)
    return shard


def laplace_rows(extended):
    row_count = extended.shape[1] - 8
    width_x = extended.shape[2]
    width_y = extended.shape[3]
    padded = jnp.pad(extended, ((0, 0), (0, 0), (4, 4), (4, 4)))

    def shifted(dz, dx, dy):
        return padded[
            :, 4 + dz : 4 + dz + row_count, 4 + dx : 4 + dx + width_x, 4 + dy : 4 + dy + width_y
        ]

    summed = 3.0 * STENCIL[0] * shifted(0, 0, 0)
    for reach in range(1, 5):
        summed = summed + STENCIL[reach] * (
            shifted(reach, 0, 0)
            + shifted(-reach, 0, 0)
            + shifted(0, reach, 0)
            + shifted(0, -reach, 0)
            + shifted(0, 0, reach)
            + shifted(0, 0, -reach)
        )
    return summed


def inject(cells, amounts, start_row, row_count, width_x, width_y):
    plane = width_x * width_y
    offset_cells = cells - start_row * plane
    inside = (offset_cells >= 0) & (offset_cells < row_count * plane)
    flat = (
        jnp.zeros((row_count * plane,), jnp.float32)
        .at[jnp.where(inside, offset_cells, 0)]
        .add(jnp.where(inside, amounts, 0.0))
    )
    return flat.reshape(row_count, width_x, width_y)


def sources_for(injections, start_row, row_count, width_x, width_y):
    return jnp.stack(
        [
            inject(cells, amounts, start_row, row_count, width_x, width_y)
            for cells, amounts in injections
        ]
    )


def advance(current, previous, coefficient, injections, first_row):
    slab_rows, width_x, width_y = (current.shape[1], current.shape[2], current.shape[3])
    extended = with_halo(current, (("ap", 1),), 4)
    sources = sources_for(injections, first_row, slab_rows, width_x, width_y)
    return 2.0 * current - previous + coefficient[None] * (laplace_rows(extended) + sources)


def march(current, previous, coefficient, injections_at, first_row):
    snapshots = []
    for t in range(STEPS):
        updated = advance(current, previous, coefficient, injections_at(t), first_row)
        previous, current = (current, updated)
        snapshots.append(current)
    return snapshots


def shards(
    forward_field,
    forward_older,
    adjoint_field,
    adjoint_newer,
    velocity,
    anchor_first,
    anchor_second,
    wavelet,
    source_cell,
    receivers,
    traces,
):
    slab_rows, width_x, width_y = (
        forward_field.shape[1],
        forward_field.shape[2],
        forward_field.shape[3],
    )
    first_row = lax.axis_index("ap") * slab_rows
    anchor = anchor_first[0] * 0
    speed_model = lax.all_gather(velocity, "shot", axis=1, tiled=True)
    window = lax.dynamic_slice(
        speed_model, (anchor, anchor_first[0], anchor_second[0]), (slab_rows, width_x, width_y)
    )
    coefficient = window * window
    f_now, f_old, a_now, a_new = (forward_field, forward_older, adjoint_field, adjoint_newer)

    def forward_source(t):
        return (source_cell, wavelet[0, t : t + 1])

    def adjoint_source(t):
        return (receivers[0], traces[0, STEPS - 1 - t])

    forward_snaps = march(
        f_now.astype(jnp.float32),
        f_old.astype(jnp.float32),
        coefficient,
        lambda t: [forward_source(t)],
        first_row,
    )
    adjoint_snaps = march(
        a_now.astype(jnp.float32),
        a_new.astype(jnp.float32),
        coefficient,
        lambda t: [adjoint_source(t)],
        first_row,
    )
    forward_states = [state[0] for state in forward_snaps]
    adjoint_states = [state[0] for state in adjoint_snaps]
    correlation = forward_states[0] * adjoint_states[STEPS - 1]
    for t in range(1, STEPS):
        correlation = correlation + forward_states[t] * adjoint_states[STEPS - 1 - t]
    shot_image = correlation / STEPS
    partial_image = lax.dynamic_update_slice(
        jnp.zeros((slab_rows, GX, GY), jnp.float32),
        shot_image,
        (anchor, anchor_first[0], anchor_second[0]),
    )
    return lax.psum_scatter(partial_image, "shot", scatter_dimension=1, tiled=True)


def solution(mesh):
    in_specs = (
        P(("groups", "shot"), "ap", None, None),
        P(("groups", "shot"), "ap", None, None),
        P(("groups", "shot"), "ap", None, None),
        P(("groups", "shot"), "ap", None, None),
        P(("groups", "ap"), "shot", None),
        P(("groups", "shot")),
        P(("groups", "shot")),
        P(("groups", "shot"), None),
        P(("groups", "shot")),
        P(("groups", "shot"), None),
        P(("groups", "shot"), None, None),
    )
    out_specs = P(("groups", "ap"), "shot", None)
    return jax.shard_map(shards, mesh=mesh, in_specs=in_specs, out_specs=out_specs, check_vma=False)
```

profile of v0, /device:TPU:0, one launch (start us, length us, event | category | flops | bytes accessed | tf_op | source)
XLA Modules:
  0.0 200.8 jit_solution(1978590393270507176)
XLA Ops:
  6.5 1.6 fusion.297
  8.2 1.4 collective-permute-start.2
  9.6 3.0 %collective-permute-start.3 = (f32[1,4,64,128]{3,2,1,0:T(8,128)}, f32[1,4,64,128]{3,2,1,0:T(8,128)S(1)}, u32[]{:S(2)}, u32[]{:S(2)}) collective-permute-start(f32[1,4,64,128]{3,2,1,0:T(8,128)} %get-tuple-element.68), channel_id=1, source_target_pairs={{0,1},{2,3},{4,5},{6,7},{8,9},{10,11},{12,13},{14,15},{16,17},{18,... | collective-permute-start | bytes 393224 | tf_op jit(solution)/shard_map/ppermute | solution.py:21
  12.6 1.6 fusion.296
  14.2 1.3 collective-permute-start
  15.5 3.7 %collective-permute-start.1 = (f32[1,4,64,128]{3,2,1,0:T(8,128)}, f32[1,4,64,128]{3,2,1,0:T(8,128)}, u32[]{:S(2)}, u32[]{:S(2)}) collective-permute-start(f32[1,4,64,128]{3,2,1,0:T(8,128)} %get-tuple-element.66), channel_id=1, source_target_pairs={{0,1},{2,3},{4,5},{6,7},{8,9},{10,11},{12,13},{14,15},{16,17},{18,... | collective-permute-start | bytes 393224 | tf_op jit(solution)/shard_map/ppermute | solution.py:21
  19.2 0.8 fusion.298
  20.0 35.7 %all_gather.3 = f32[8,128,192]{2,1,0:T(8,128)S(1)} all-gather(f32[8,16,192]{2,1,0:T(8,128)} %param.23), channel_id=1, replica_groups=mesh['groups'=2,'shot'=8,'ap'=2] {'shot'}, dimensions={1}, use_global_device_ids=true | all-gather | bytes 884736 | tf_op jit(solution)/shard_map/all_gather | solution.py:108
  57.9 2.0 %scatter_custom_fusion = f32[65536]{0:T(1024)S(1)} fusion(s32[256]{0:T(256)S(1)} %bitcast.71, f32[256]{0:T(256)S(1)} %get-tuple-element.76, f32[]{:T(128)} %constant.97.clone.1), kind=kCustom, calls=%fused_computation.449 | custom fusion | flops 256 | bytes 262148 | tf_op jit(solution)/shard_map/scatter-add | solution.py:58
  59.9 2.0 %scatter_custom_fusion.1 = f32[65536]{0:T(1024)S(1)} fusion(s32[256]{0:T(256)S(1)} %bitcast.72, f32[256]{0:T(256)S(1)} %get-tuple-element.75, f32[]{:T(128)} %constant.97.clone.1), kind=kCustom, calls=%fused_computation.447 | custom fusion | flops 256 | bytes 262148 | tf_op jit(solution)/shard_map/scatter-add | solution.py:58
  61.9 2.0 %scatter_custom_fusion.2 = f32[65536]{0:T(1024)S(1)} fusion(s32[256]{0:T(256)S(1)} %bitcast.73, f32[256]{0:T(256)S(1)} %get-tuple-element.74, f32[]{:T(128)} %constant.97.clone.1), kind=kCustom, calls=%fused_computation.445 | custom fusion | flops 256 | bytes 262148 | tf_op jit(solution)/shard_map/scatter-add | solution.py:58
  64.5 0.7 fusion.299
  65.2 1.3 fusion.289
  66.5 1.3 fusion.287
  67.8 0.7 broadcast.149.clone.1
  68.5 2.6 %fusion.285 = f32[65536]{0:T(1024)} fusion(f32[65536]{0:T(1024)} %broadcast.149.clone.1, s32[]{:T(128)} %bitcast.5, f32[1,1]{1,0:T(1,128)} %get-tuple-element.80, s32[1]{0:T(128)S(6)} %copy.23, s32[1]{0:T(128)} %bitcast.3), kind=kLoop, calls=%fused_computation.462 | loop fusion | flops 13 | bytes 2052 | tf_op jit(solution)/shard_map/scatter-add | solution.py:58
  71.1 0.7 broadcast.149.clone
  71.8 2.5 %fusion.283 = f32[65536]{0:T(1024)} fusion(f32[65536]{0:T(1024)} %broadcast.149.clone, s32[]{:T(128)} %bitcast.5, f32[1,1]{1,0:T(1,128)} %get-tuple-element.79, s32[1]{0:T(128)S(6)} %copy.23, s32[1]{0:T(128)} %bitcast.3), kind=kLoop, calls=%fused_computation.459 | loop fusion | flops 13 | bytes 2052 | tf_op jit(solution)/shard_map/scatter-add | solution.py:58
  74.4 2.6 %scatter_custom_fusion.3 = f32[65536]{0:T(1024)} fusion(s32[256]{0:T(256)S(1)} %bitcast.74, f32[256]{0:T(256)S(1)} %get-tuple-element.73, f32[]{:T(128)} %constant.97.clone.1), kind=kCustom, calls=%fused_computation.443 | custom fusion | flops 256 | bytes 262148 | tf_op jit(solution)/shard_map/scatter-add | solution.py:58
  77.0 0.0 copy-start.12
  77.0 0.4 select_maximum_fusion.12
  77.4 0.2 copy-done.11
  77.6 0.1 copy-done.12
  77.7 0.3 copy-done.13
  78.0 2.3 %fusion.206 = f32[1,8,64,128]{3,2,1,0:T(8,128)S(1)} fusion(f32[1,8,64,128]{3,2,1,0:T(8,128)S(1)} %bitcast.64, f32[1,8,64,128]{3,2,1,0:T(8,128)S(1)} %convert_element_type.23, f32[1,4,64,128]{3,2,1,0:T(8,128)} %copy-done.12, f32[1,4,64,128]{3,2,1,0:T(8,128)} %copy-done.11, f32[1,16,72,136]{3,2,1,0:T(8,128)S(1)} %select_maximum_fusion.12, ...), kind=kLoop, calls=%fused_computation.326 | loop fusion | flops 2883584 | bytes 5636104 | tf_op jit(solution)/shard_map/add | solution.py:76
  80.3 0.0 copy-start.14
  80.4 1.4 collective-permute-start.4
  81.8 3.0 %collective-permute-start.5 = (f32[1,4,64,128]{3,2,1,0:T(8,128)S(1)}, f32[1,4,64,128]{3,2,1,0:T(8,128)S(1)}, u32[]{:S(2)}, u32[]{:S(2)}) collective-permute-start(f32[1,4,64,128]{3,2,1,0:T(8,128)S(1)} %get-tuple-element.58), channel_id=1, source_target_pairs={{0,1},{2,3},{4,5},{6,7},{8,9},{10,11},{12,13},{14,15},{16,17},{18,... | collective-permute-start | bytes 393224 | tf_op jit(solution)/shard_map/ppermute | solution.py:21
  84.9 0.0 collective-permute-done
  84.9 1.3 select_maximum_fusion.14
  86.2 2.2 %fusion.237 = f32[1,8,64,128]{3,2,1,0:T(8,128)S(1)} fusion(f32[1,8,64,128]{3,2,1,0:T(8,128)S(1)} %bitcast.65, f32[1,8,64,128]{3,2,1,0:T(8,128)S(1)} %convert_element_type.21, f32[1,4,64,128]{3,2,1,0:T(8,128)} %collective-permute-done.1, f32[1,4,64,128]{3,2,1,0:T(8,128)S(1)} %collective-permute-done, f32[1,16,72,136]{3,2,1,0:T(8,128)S(1)} %select_maximum_fusion.14, ...), kind=kLoop, calls=%fused_computation.357 | loop fusion | flops 2883584 | bytes 5636104 | tf_op jit(solution)/shard_map/add | solution.py:76
  88.5 1.3 collective-permute-start.10
  89.8 3.0 %collective-permute-start.11 = (f32[1,4,64,128]{3,2,1,0:T(8,128)S(1)}, f32[1,4,64,128]{3,2,1,0:T(8,128)S(1)}, u32[]{:S(2)}, u32[]{:S(2)}) collective-permute-start(f32[1,4,64,128]{3,2,1,0:T(8,128)S(1)} %get-tuple-element.64), channel_id=1, source_target_pairs={{0,1},{2,3},{4,5},{6,7},{8,9},{10,11},{12,13},{14,15},{16,17},{18,... | collective-permute-start | bytes 393224 | tf_op jit(solution)/shard_map/ppermute | solution.py:21
  92.8 0.0 collective-permute-done.4
  92.8 0.0 collective-permute-done.5
  92.8 0.4 select_maximum_fusion.10
  93.2 1.2 fusion.175
  94.4 1.3 collective-permute-start.6
  95.7 3.2 %collective-permute-start.7 = (f32[1,4,64,128]{3,2,1,0:T(8,128)S(1)}, f32[1,4,64,128]{3,2,1,0:T(8,128)S(1)}, u32[]{:S(2)}, u32[]{:S(2)}) collective-permute-start(f32[1,4,64,128]{3,2,1,0:T(8,128)S(1)} %get-tuple-element.56), channel_id=1, source_target_pairs={{0,1},{2,3},{4,5},{6,7},{8,9},{10,11},{12,13},{14,15},{16,17},{18,... | collective-permute-start | bytes 393224 | tf_op jit(solution)/shard_map/ppermute | solution.py:21
  98.9 0.0 collective-permute-done.11
  99.0 0.4 select_maximum_fusion.4
  99.3 1.2 fusion.79
  100.5 1.3 collective-permute-start.12
  101.8 3.0 %collective-permute-start.13 = (f32[1,4,64,128]{3,2,1,0:T(8,128)S(1)}, f32[1,4,64,128]{3,2,1,0:T(8,128)S(1)}, u32[]{:S(2)}, u32[]{:S(2)}) collective-permute-start(f32[1,4,64,128]{3,2,1,0:T(8,128)S(1)} %get-tuple-element.62), channel_id=1, source_target_pairs={{0,1},{2,3},{4,5},{6,7},{8,9},{10,11},{12,13},{14,15},{16,17},{18,... | collective-permute-start | bytes 393224 | tf_op jit(solution)/shard_map/ppermute | solution.py:21
  104.9 0.0 collective-permute-done.7
  104.9 0.4 select_maximum_fusion.8
  105.3 1.2 fusion.144
  106.5 1.3 collective-permute-start.8
  107.8 3.0 %collective-permute-start.9 = (f32[1,4,64,128]{3,2,1,0:T(8,128)S(1)}, f32[1,4,64,128]{3,2,1,0:T(8,128)S(1)}, u32[]{:S(2)}, u32[]{:S(2)}) collective-permute-start(f32[1,4,64,128]{3,2,1,0:T(8,128)S(1)} %get-tuple-element.53), channel_id=1, source_target_pairs={{0,1},{2,3},{4,5},{6,7},{8,9},{10,11},{12,13},{14,15},{16,17},{18,... | collective-permute-start | bytes 393224 | tf_op jit(solution)/shard_map/ppermute | solution.py:21
  110.9 0.4 select_maximum_fusion.2
  111.3 2.1 %fusion.48 = f32[1,8,64,128]{3,2,1,0:T(8,128)S(1)} fusion(f32[1,8,64,128]{3,2,1,0:T(8,128)} %bitcast.20, f32[1,8,64,128]{3,2,1,0:T(8,128)S(1)} %fusion.79, f32[1,4,64,128]{3,2,1,0:T(8,128)S(1)} %collective-permute-done.13, f32[1,4,64,128]{3,2,1,0:T(8,128)S(1)} %collective-permute-done.12, f32[1,16,72,136]{3,2,1,0:T(8,128)S(1)} %select_maximum_fusion.2, ...), kind=kLoop, calls=%fused_computation.168 | loop fusion | flops 2818048 | bytes 5767176 | tf_op jit(solution)/shard_map/add | solution.py:76
  113.4 1.3 collective-permute-start.14
  114.7 3.0 %collective-permute-start.15 = (f32[1,4,64,128]{3,2,1,0:T(8,128)S(1)}, f32[1,4,64,128]{3,2,1,0:T(8,128)S(1)}, u32[]{:S(2)}, u32[]{:S(2)}) collective-permute-start(f32[1,4,64,128]{3,2,1,0:T(8,128)S(1)} %get-tuple-element.59), channel_id=1, source_target_pairs={{0,1},{2,3},{4,5},{6,7},{8,9},{10,11},{12,13},{14,15},{16,17},{18,... | collective-permute-start | bytes 393224 | tf_op jit(solution)/shard_map/ppermute | solution.py:21
  117.8 0.4 select_maximum_fusion.6
  118.2 0.5 collective-permute-done.15
  118.7 0.4 select_maximum_fusion
  119.2 0.2 copy-done.10
  119.4 5.3 %fusion.273 = f32[8,64,128]{2,1,0:T(8,128)} fusion(f32[1,8,64,128]{3,2,1,0:T(8,128)S(1)} %fusion.206, f32[1,8,64,128]{3,2,1,0:T(8,128)} %bitcast.22, f32[1,16,72,136]{3,2,1,0:T(8,128)S(1)} %select_maximum_fusion, f32[1,8,64,128]{3,2,1,0:T(8,128)} %copy-done.2, f32[1,4,64,128]{3,2,1,0:T(8,128)} %copy-done.10, f32[1,4,64,128]{3,2,1,0:T(8,128)} %copy-done.9, ...), kind=kLoop, calls=%fused_computation.442 | loop fusion | flops 6094848 | bytes 11534344 | tf_op jit(solution)/shard_map/div | solution.py:140
  124.7 0.1 broadcast_in_dim.43
  124.8 0.9 copy-done.6
  125.6 3.9 %dynamic_update_slice.3 = f32[8,128,192]{2,1,0:T(8,128)S(1)} dynamic-update-slice(f32[8,128,192]{2,1,0:T(8,128)S(1)} %broadcast_in_dim.43, f32[8,64,128]{2,1,0:T(8,128)S(1)} %copy-done.6, s32[]{:T(128)} %constant.99.clone.1, s32[]{:T(128)S(6)} %select_n.74, s32[]{:T(128)S(6)} %select_n.75) | dynamic-update-slice | bytes 524292 | tf_op jit(solution)/shard_map/dynamic_update_slice | solution.py:141
  129.6 1.0 copy-done.3
  130.6 0.0 reduce-scatter.2.cloned.1.call-update
  130.6 63.4 %reduce-scatter.2.cloned.1.call-done = f32[8,16,192]{2,1,0:T(8,128)} async-done(((f32[8,128,192]{2,1,0:T(8,128)}), f32[8,16,192]{2,1,0:T(8,128)}) %reduce-scatter.2.cloned.1.call-update) | async-done | bytes 98320 | tf_op jit(solution)/shard_map/reduce_scatter | solution.py:146
  (50 shorter events, 0.3 us)
Async XLA Ops:
  6.5 49.3 %copy-start.4 = (bf16[1,8,64,128]{3,2,1,0:T(8,128)(2,1)S(1)}, bf16[1,8,64,128]{3,2,1,0:T(8,128)(2,1)}, u32[]{:S(2)}) copy-start(bf16[1,8,64,128]{3,2,1,0:T(8,128)(2,1)} %param.21) | copy-start | bytes 393220
  6.5 49.2 %copy-start.16 = (s32[1,256]{1,0:T(1,128)S(1)}, s32[1,256]{1,0:T(1,128)}, u32[]{:S(2)}) copy-start(s32[1,256]{1,0:T(1,128)} %param.28) | copy-start | bytes 3076
  6.5 187.4 %reduce-scatter.2.cloned.1.call-start = ((), (), s32[]{:S(2)}) async-start(), calls=%async_computation.1 | async-start | bytes 1179648 | tf_op jit(solution)/shard_map/reduce_scatter | solution.py:146
  8.2 47.7 %copy-start.5 = (bf16[1,8,64,128]{3,2,1,0:T(8,128)(2,1)S(1)}, bf16[1,8,64,128]{3,2,1,0:T(8,128)(2,1)}, u32[]{:S(2)}) copy-start(bf16[1,8,64,128]{3,2,1,0:T(8,128)(2,1)} %param.19) | copy-start | bytes 393220
  8.2 68.8 %collective-permute-start.2 = (f32[1,4,64,128]{3,2,1,0:T(8,128)}, f32[1,4,64,128]{3,2,1,0:T(8,128)S(1)}, u32[]{:S(2)}, u32[]{:S(2)}) collective-permute-start(f32[1,4,64,128]{3,2,1,0:T(8,128)} %get-tuple-element.67), channel_id=1, source_target_pairs={{1,0},{3,2},{5,4},{7,6},{9,8},{11,10},{13,12},{15,14},{17,16},{19,... | collective-permute-start | bytes 393224 | tf_op jit(solution)/shard_map/ppermute | solution.py:22
  9.6 67.4 %collective-permute-start.3 = (f32[1,4,64,128]{3,2,1,0:T(8,128)}, f32[1,4,64,128]{3,2,1,0:T(8,128)S(1)}, u32[]{:S(2)}, u32[]{:S(2)}) collective-permute-start(f32[1,4,64,128]{3,2,1,0:T(8,128)} %get-tuple-element.68), channel_id=1, source_target_pairs={{0,1},{2,3},{4,5},{6,7},{8,9},{10,11},{12,13},{14,15},{16,17},{18,... | collective-permute-start | bytes 393224 | tf_op jit(solution)/shard_map/ppermute | solution.py:21
  14.2 70.6 %collective-permute-start = (f32[1,4,64,128]{3,2,1,0:T(8,128)}, f32[1,4,64,128]{3,2,1,0:T(8,128)S(1)}, u32[]{:S(2)}, u32[]{:S(2)}) collective-permute-start(f32[1,4,64,128]{3,2,1,0:T(8,128)} %get-tuple-element.65), channel_id=1, source_target_pairs={{1,0},{3,2},{5,4},{7,6},{9,8},{11,10},{13,12},{15,14},{17,16},{19,... | collective-permute-start | bytes 393224 | tf_op jit(solution)/shard_map/ppermute | solution.py:22
  15.5 69.3 %collective-permute-start.1 = (f32[1,4,64,128]{3,2,1,0:T(8,128)}, f32[1,4,64,128]{3,2,1,0:T(8,128)}, u32[]{:S(2)}, u32[]{:S(2)}) collective-permute-start(f32[1,4,64,128]{3,2,1,0:T(8,128)} %get-tuple-element.66), channel_id=1, source_target_pairs={{0,1},{2,3},{4,5},{6,7},{8,9},{10,11},{12,13},{14,15},{16,17},{18,... | collective-permute-start | bytes 393224 | tf_op jit(solution)/shard_map/ppermute | solution.py:21
  20.0 44.4 %copy-start.15 = (f32[1,4]{1,0:T(1,128)S(1)}, f32[1,4]{1,0:T(1,128)}, u32[]{:S(2)}) copy-start(f32[1,4]{1,0:T(1,128)} %param.26) | copy-start | bytes 52
  55.8 55.5 %copy-start = (f32[8,128,192]{2,1,0:T(8,128)}, f32[8,128,192]{2,1,0:T(8,128)S(1)}, u32[]{:S(2)}) copy-start(f32[8,128,192]{2,1,0:T(8,128)S(1)} %all_gather.3) | copy-start | bytes 2359300
  77.0 1.0 copy-start.13
  77.0 0.6 copy-start.11
  77.0 0.7 copy-start.12
  80.3 5.8 %copy-start.14 = (bf16[1,8,64,128]{3,2,1,0:T(8,128)(2,1)S(1)}, bf16[1,8,64,128]{3,2,1,0:T(8,128)(2,1)}, u32[]{:S(2)}) copy-start(bf16[1,8,64,128]{3,2,1,0:T(8,128)(2,1)} %param.20) | copy-start | bytes 393220
  80.4 12.4 %collective-permute-start.4 = (f32[1,4,64,128]{3,2,1,0:T(8,128)S(1)}, f32[1,4,64,128]{3,2,1,0:T(8,128)S(1)}, u32[]{:S(2)}, u32[]{:S(2)}) collective-permute-start(f32[1,4,64,128]{3,2,1,0:T(8,128)S(1)} %get-tuple-element.57), channel_id=1, source_target_pairs={{1,0},{3,2},{5,4},{7,6},{9,8},{11,10},{13,12},{15,14},{17,16},{19,... | collective-permute-start | bytes 393224 | tf_op jit(solution)/shard_map/ppermute | solution.py:22
  81.8 11.0 %collective-permute-start.5 = (f32[1,4,64,128]{3,2,1,0:T(8,128)S(1)}, f32[1,4,64,128]{3,2,1,0:T(8,128)S(1)}, u32[]{:S(2)}, u32[]{:S(2)}) collective-permute-start(f32[1,4,64,128]{3,2,1,0:T(8,128)S(1)} %get-tuple-element.58), channel_id=1, source_target_pairs={{0,1},{2,3},{4,5},{6,7},{8,9},{10,11},{12,13},{14,15},{16,17},{18,... | collective-permute-start | bytes 393224 | tf_op jit(solution)/shard_map/ppermute | solution.py:21
  88.5 10.5 %collective-permute-start.10 = (f32[1,4,64,128]{3,2,1,0:T(8,128)S(1)}, f32[1,4,64,128]{3,2,1,0:T(8,128)S(1)}, u32[]{:S(2)}, u32[]{:S(2)}) collective-permute-start(f32[1,4,64,128]{3,2,1,0:T(8,128)S(1)} %get-tuple-element.63), channel_id=1, source_target_pairs={{1,0},{3,2},{5,4},{7,6},{9,8},{11,10},{13,12},{15,14},{17,16},{19,... | collective-permute-start | bytes 393224 | tf_op jit(solution)/shard_map/ppermute | solution.py:22
  89.8 9.2 %collective-permute-start.11 = (f32[1,4,64,128]{3,2,1,0:T(8,128)S(1)}, f32[1,4,64,128]{3,2,1,0:T(8,128)S(1)}, u32[]{:S(2)}, u32[]{:S(2)}) collective-permute-start(f32[1,4,64,128]{3,2,1,0:T(8,128)S(1)} %get-tuple-element.64), channel_id=1, source_target_pairs={{0,1},{2,3},{4,5},{6,7},{8,9},{10,11},{12,13},{14,15},{16,17},{18,... | collective-permute-start | bytes 393224 | tf_op jit(solution)/shard_map/ppermute | solution.py:21
  94.4 10.5 %collective-permute-start.6 = (f32[1,4,64,128]{3,2,1,0:T(8,128)S(1)}, f32[1,4,64,128]{3,2,1,0:T(8,128)S(1)}, u32[]{:S(2)}, u32[]{:S(2)}) collective-permute-start(f32[1,4,64,128]{3,2,1,0:T(8,128)S(1)} %get-tuple-element.55), channel_id=1, source_target_pairs={{1,0},{3,2},{5,4},{7,6},{9,8},{11,10},{13,12},{15,14},{17,16},{19,... | collective-permute-start | bytes 393224 | tf_op jit(solution)/shard_map/ppermute | solution.py:22
  95.7 9.2 %collective-permute-start.7 = (f32[1,4,64,128]{3,2,1,0:T(8,128)S(1)}, f32[1,4,64,128]{3,2,1,0:T(8,128)S(1)}, u32[]{:S(2)}, u32[]{:S(2)}) collective-permute-start(f32[1,4,64,128]{3,2,1,0:T(8,128)S(1)} %get-tuple-element.56), channel_id=1, source_target_pairs={{0,1},{2,3},{4,5},{6,7},{8,9},{10,11},{12,13},{14,15},{16,17},{18,... | collective-permute-start | bytes 393224 | tf_op jit(solution)/shard_map/ppermute | solution.py:21
  100.5 10.3 %collective-permute-start.12 = (f32[1,4,64,128]{3,2,1,0:T(8,128)S(1)}, f32[1,4,64,128]{3,2,1,0:T(8,128)S(1)}, u32[]{:S(2)}, u32[]{:S(2)}) collective-permute-start(f32[1,4,64,128]{3,2,1,0:T(8,128)S(1)} %get-tuple-element.61), channel_id=1, source_target_pairs={{1,0},{3,2},{5,4},{7,6},{9,8},{11,10},{13,12},{15,14},{17,16},{19,... | collective-permute-start | bytes 393224 | tf_op jit(solution)/shard_map/ppermute | solution.py:22
  101.8 9.0 %collective-permute-start.13 = (f32[1,4,64,128]{3,2,1,0:T(8,128)S(1)}, f32[1,4,64,128]{3,2,1,0:T(8,128)S(1)}, u32[]{:S(2)}, u32[]{:S(2)}) collective-permute-start(f32[1,4,64,128]{3,2,1,0:T(8,128)S(1)} %get-tuple-element.62), channel_id=1, source_target_pairs={{0,1},{2,3},{4,5},{6,7},{8,9},{10,11},{12,13},{14,15},{16,17},{18,... | collective-permute-start | bytes 393224 | tf_op jit(solution)/shard_map/ppermute | solution.py:21
  106.5 11.4 %copy-start.1 = (f32[1,8,64,128]{3,2,1,0:T(8,128)}, f32[1,8,64,128]{3,2,1,0:T(8,128)S(1)}, u32[]{:S(2)}) copy-start(f32[1,8,64,128]{3,2,1,0:T(8,128)S(1)} %fusion.144) | copy-start | bytes 786436
  106.5 11.3 %collective-permute-start.8 = (f32[1,4,64,128]{3,2,1,0:T(8,128)S(1)}, f32[1,4,64,128]{3,2,1,0:T(8,128)S(1)}, u32[]{:S(2)}, u32[]{:S(2)}) collective-permute-start(f32[1,4,64,128]{3,2,1,0:T(8,128)S(1)} %get-tuple-element.54), channel_id=1, source_target_pairs={{1,0},{3,2},{5,4},{7,6},{9,8},{11,10},{13,12},{15,14},{17,16},{19,... | collective-permute-start | bytes 393224 | tf_op jit(solution)/shard_map/ppermute | solution.py:22
  107.8 10.0 %collective-permute-start.9 = (f32[1,4,64,128]{3,2,1,0:T(8,128)S(1)}, f32[1,4,64,128]{3,2,1,0:T(8,128)S(1)}, u32[]{:S(2)}, u32[]{:S(2)}) collective-permute-start(f32[1,4,64,128]{3,2,1,0:T(8,128)S(1)} %get-tuple-element.53), channel_id=1, source_target_pairs={{0,1},{2,3},{4,5},{6,7},{8,9},{10,11},{12,13},{14,15},{16,17},{18,... | collective-permute-start | bytes 393224 | tf_op jit(solution)/shard_map/ppermute | solution.py:21
  113.4 5.3 %copy-start.2 = (f32[1,8,64,128]{3,2,1,0:T(8,128)}, f32[1,8,64,128]{3,2,1,0:T(8,128)S(1)}, u32[]{:S(2)}) copy-start(f32[1,8,64,128]{3,2,1,0:T(8,128)S(1)} %fusion.48) | copy-start | bytes 786436
  113.4 4.8 %collective-permute-start.14 = (f32[1,4,64,128]{3,2,1,0:T(8,128)S(1)}, f32[1,4,64,128]{3,2,1,0:T(8,128)S(1)}, u32[]{:S(2)}, u32[]{:S(2)}) collective-permute-start(f32[1,4,64,128]{3,2,1,0:T(8,128)S(1)} %get-tuple-element.60), channel_id=1, source_target_pairs={{1,0},{3,2},{5,4},{7,6},{9,8},{11,10},{13,12},{15,14},{17,16},{19,... | collective-permute-start | bytes 393224 | tf_op jit(solution)/shard_map/ppermute | solution.py:22
  114.7 4.0 %collective-permute-start.15 = (f32[1,4,64,128]{3,2,1,0:T(8,128)S(1)}, f32[1,4,64,128]{3,2,1,0:T(8,128)S(1)}, u32[]{:S(2)}, u32[]{:S(2)}) collective-permute-start(f32[1,4,64,128]{3,2,1,0:T(8,128)S(1)} %get-tuple-element.59), channel_id=1, source_target_pairs={{0,1},{2,3},{4,5},{6,7},{8,9},{10,11},{12,13},{14,15},{16,17},{18,... | collective-permute-start | bytes 393224 | tf_op jit(solution)/shard_map/ppermute | solution.py:21
  117.8 1.3 copy-start.7
  117.8 1.3 copy-start.8
  118.2 0.9 copy-start.9
  118.7 0.7 copy-start.10
  124.7 1.0 copy-start.6
  129.6 1.0 copy-start.3
Sparse Core Ops, SparseCore 0:
  130.7 63.1 reduce-scatter.1
where the time goes:
time: 201 us
  waiting for transfers between devices  63.9 us (32%)
  other arithmetic  35.9 us (18%)
  starting transfers between devices  35.7 us (18%)
  blocking collectives  35.7 us (18%)
  between operations  16.5 us (8%)
  local copies, waits for them, and re-layouts  13.1 us (7%)
    reduce_scatter x1, waiting for transfers between devices, shards(): lax.psum_scatter(partial_image, 'shot', scatter_dimension=1, tiled=True)  63.4 us
    all_gather x1, blocking collectives, shards(): speed_model = lax.all_gather(velocity, 'shot', axis=1, tiled=True)  35.7 us
    ppermute x8, starting transfers between devices, with_halo(): before = lax.ppermute(last, axis, up)  25.2 us
    scatter-add x8, other arithmetic, inject(): flat = jnp.zeros((row_count * plane,), jnp.float32).at[jnp.where(inside,...  16.4 us
    ppermute x8, starting transfers between devices, with_halo(): after = lax.ppermute(initial, axis, down)  10.6 us
    add x6, other arithmetic, advance(): 2.0 * current - previous  10.2 us
    div x1, other arithmetic, shards(): shot_image = correlation / STEPS  5.29 us
  transfers between devices with their start and end apart: 17, of which 2 were waited for; matrix products, arithmetic and copies ran while one was open for 17% of the time, Pallas kernels for 0%

commit v1 on v0

--- a/solution.py
+++ b/solution.py
@@ -1,6 +1,8 @@
 import jax
 import jax.numpy as jnp
 from jax import lax
+from jax.experimental import pallas as pl
+from jax.experimental.pallas import tpu as pltpu
 from jax.sharding import PartitionSpec as P
 
 STEPS = 4
@@ -146,7 +148,343 @@
     return lax.psum_scatter(partial_image, "shot", scatter_dimension=1, tiled=True)
 
 
+SLAB, AX, AY = 8, 64, 128
+COLUMNS, LEVELS = 2, 4
+SHOTS = COLUMNS * LEVELS
+ROWS = GX // SHOTS
+TAIL = GY - AY
+PAD = 8
+REACH = 4
+MESH = pl.DeviceIdType.MESH
+
+
+def window_kernel(
+    a_ref,
+    b_ref,
+    wavelet_ref,
+    source_ref,
+    receivers_ref,
+    traces_ref,
+    forward_ref,
+    forward_older_ref,
+    adjoint_ref,
+    adjoint_newer_ref,
+    velocity_ref,
+    out_ref,
+    state,
+    model,
+    coefficient,
+    injected,
+    placed,
+    outgoing,
+    incoming,
+    offsets,
+    offset_tile,
+    halo_send,
+    halo_recv,
+    model_send,
+    model_recv,
+    image_send,
+    image_recv,
+    offset_send,
+    offset_recv,
+):
+    half = lax.axis_index("ap")
+    me = lax.axis_index("shot")
+    level, column = me // COLUMNS, me % COLUMNS
+
+    barrier = pltpu.get_barrier_semaphore()
+    pl.semaphore_signal(barrier, inc=1, device_id={"ap": 1 - half}, device_id_type=MESH)
+    for away in range(1, SHOTS):
+        pl.semaphore_signal(
+            barrier, inc=1, device_id={"shot": (me + away) % SHOTS}, device_id_type=MESH
+        )
+
+    a = a_ref[0]
+    b = b_ref[0]
+    lane = lax.broadcasted_iota(jnp.int32, (1, AY), 1)
+
+    mine = pl.ds(pl.multiple_of(me * ROWS, ROWS), ROWS)
+    for z in range(SLAB):
+        model[z, mine, :] = velocity_ref[z, :, 0:AY]
+    for z in range(SLAB // 2):
+        model[SLAB + z, mine, :] = jnp.concatenate(
+            [velocity_ref[z, :, AY:GY], velocity_ref[z + SLAB // 2, :, AY:GY]], axis=1
+        )
+    offset_tile[...] = jnp.full((8, AY), b, jnp.int32)
+
+    pl.semaphore_wait(barrier, SHOTS)
+
+    def model_copy(block, slot, target):
+        rows = pl.ds(pl.multiple_of(block * ROWS, ROWS), ROWS)
+        return pltpu.make_async_remote_copy(
+            src_ref=model.at[:, rows, :],
+            dst_ref=model.at[:, rows, :],
+            send_sem=model_send.at[slot],
+            recv_sem=model_recv.at[block],
+            device_id={"shot": target},
+            device_id_type=MESH,
+        )
+
+    across = level * COLUMNS + 1 - column
+    model_copies = []
+    for away in range(1, LEVELS):
+        copy = model_copy(me, away, (level + away) % LEVELS * COLUMNS + column)
+        copy.start()
+        model_copies.append(copy)
+    copy = model_copy(me, 0, across)
+    copy.start()
+    model_copies.append(copy)
+
+    offset_copies = []
+    for away in range(1, SHOTS):
+        copy = pltpu.make_async_remote_copy(
+            src_ref=offset_tile,
+            dst_ref=offsets.at[me],
+            send_sem=offset_send.at[away],
+            recv_sem=offset_recv.at[away],
+            device_id={"shot": (me + away) % SHOTS},
+            device_id_type=MESH,
+        )
+        copy.start()
+        offset_copies.append(copy)
+    offsets[me] = offset_tile[...]
+
+    outer = pl.ds((REACH + SLAB) * (half), REACH)
+    inner = pl.ds(PAD, AX)
+    for f, (older, now) in enumerate(
+        ((forward_older_ref, forward_ref), (adjoint_newer_ref, adjoint_ref))
+    ):
+        for k in range(1, STEPS + 1):
+
+            def clear(z, carry):
+                state[f, k, z + REACH, 0:PAD, :] = jnp.zeros((PAD, AY), jnp.float32)
+                state[f, k, z + REACH, PAD + AX :, :] = jnp.zeros((PAD, AY), jnp.float32)
+                return carry
+
+            lax.fori_loop(0, SLAB, clear, 0)
+            state[f, k, outer, inner, :] = jnp.zeros((REACH, AX, AY), jnp.float32)
+
+        def load(z, carry):
+            state[f, 0, z + REACH, inner, :] = older[0, z].astype(jnp.float32)
+            state[f, 1, z + REACH, inner, :] = now[0, z].astype(jnp.float32)
+            return carry
+
+        lax.fori_loop(0, SLAB, load, 0)
+
+    def halo_copy(f, k):
+        return pltpu.make_async_remote_copy(
+            src_ref=state.at[f, k, pl.ds(2 * REACH - REACH * half, REACH), inner, :],
+            dst_ref=state.at[f, k, pl.ds((REACH + SLAB) * half, REACH), inner, :],
+            send_sem=halo_send.at[f, k - 1],
+            recv_sem=halo_recv.at[f, k - 1],
+            device_id={"ap": 1 - half},
+            device_id_type=MESH,
+        )
+
+    halos = {}
+    for f in range(2):
+        halos[f, 1] = halo_copy(f, 1)
+        halos[f, 1].start()
+
+    cells = receivers_ref[...]
+    count = cells.shape[1]
+    row_of = cells // AY - half * (SLAB * AX)
+    lane_of = cells % AY
+    hot_rows = jnp.where(
+        lax.broadcasted_iota(jnp.int32, (SLAB * AX, count), 0) == row_of, 1.0, 0.0
+    ).astype(jnp.bfloat16)
+    hot_lanes = lax.broadcasted_iota(jnp.int32, (AY, count), 0) == lane_of
+    for k in range(STEPS):
+        amounts = jnp.where(hot_lanes, traces_ref[0, STEPS - 1 - k : STEPS - k, :], 0.0)
+        upper = amounts.astype(jnp.bfloat16)
+        lower = (amounts - upper.astype(jnp.float32)).astype(jnp.bfloat16)
+        both = lax.dot_general(
+            hot_rows,
+            jnp.concatenate([upper, lower], axis=0),
+            (((1,), (1,)), ((), ())),
+            preferred_element_type=jnp.float32,
+        )
+        injected[k] = (both[:, :AY] + both[:, AY:]).reshape(SLAB, AX, AY)
+
+    def blank(z, carry):
+        placed[z, 0:AX, :] = jnp.zeros((AX, AY), jnp.float32)
+        placed[z, 2 * AX :, :] = jnp.zeros((GX - AX, AY), jnp.float32)
+        return carry
+
+    lax.fori_loop(0, SLAB, blank, 0)
+
+    for away in range(1, LEVELS):
+        block = (level + LEVELS - away) % LEVELS * COLUMNS + column
+        model_copy(block, 0, across).wait_recv()
+        copy = model_copy(block, LEVELS - 1 + away, across)
+        copy.start()
+        model_copies.append(copy)
+    for away in range(LEVELS):
+        block = (level + LEVELS - away) % LEVELS * COLUMNS + 1 - column
+        model_copy(block, 0, across).wait_recv()
+
+    def square(z, carry):
+        rows = pl.ds(a, AX)
+        for part in range(2):
+            tail = model[SLAB + z, rows, :]
+            if part:
+                tail = pltpu.roll(tail, TAIL, 1)
+            joined = jnp.where(lane >= b, model[z + part * (SLAB // 2), rows, :], tail)
+            window = pltpu.roll(joined, (AY - b) % AY, 1)
+            coefficient[z + part * (SLAB // 2)] = window * window
+        return carry
+
+    lax.fori_loop(0, SLAB // 2, square, 0)
+
+    flat = (
+        lax.broadcasted_iota(jnp.int32, (AX, AY), 0) * AY
+        + lax.broadcasted_iota(jnp.int32, (AX, AY), 1)
+    )
+
+    def layers(f, k, first):
+        def layer(i, carry):
+            z = first + i
+            slot = z + REACH
+            centre = state[f, k + 1, slot, inner, :]
+            total = (3.0 * STENCIL[0]) * centre
+            for reach in range(1, REACH + 1):
+                near = state[f, k + 1, slot + reach, inner, :]
+                near = near + state[f, k + 1, slot - reach, inner, :]
+                near = near + state[f, k + 1, slot, pl.ds(PAD + reach, AX), :]
+                near = near + state[f, k + 1, slot, pl.ds(PAD - reach, AX), :]
+                near = near + jnp.where(lane >= reach, pltpu.roll(centre, reach, 1), 0.0)
+                near = near + jnp.where(
+                    lane < AY - reach, pltpu.roll(centre, AY - reach, 1), 0.0
+                )
+                total = total + STENCIL[reach] * near
+            if f == 0:
+                here = source_ref[0] - (z + half * SLAB) * (AX * AY)
+                total = total + jnp.where(flat == here, wavelet_ref[0, k], 0.0)
+            else:
+                total = total + injected[k, z]
+            state[f, k + 2, slot, inner, :] = (
+                2.0 * centre - state[f, k, slot, inner, :] + coefficient[z] * total
+            )
+            return carry
+
+        lax.fori_loop(0, REACH, layer, 0)
+
+    far, edge = REACH * half, REACH - REACH * half
+    for k in range(STEPS):
+        layers(0, k, far)
+        layers(1, k, far)
+        for f in range(2):
+            halos[f, k + 1].wait_recv()
+            layers(f, k, edge)
+            if k + 1 < STEPS:
+                halos[f, k + 2] = halo_copy(f, k + 2)
+                halos[f, k + 2].start()
+
+    def correlate(z, carry):
+        slot = z + REACH
+        image = state[0, 2, slot, inner, :] * state[1, STEPS + 1, slot, inner, :]
+        for t in range(1, STEPS):
+            image = image + state[0, t + 2, slot, inner, :] * state[1, STEPS + 1 - t, slot, inner, :]
+        placed[z, pl.ds(AX, AX), :] = pltpu.roll(image * (1.0 / STEPS), b, 1)
+        return carry
+
+    lax.fori_loop(0, SLAB, correlate, 0)
+
+    image_copies = []
+    for away in range(1, SHOTS):
+        owner = (me + away) % SHOTS
+        outgoing[away] = placed[:, pl.ds(AX - a + owner * ROWS, ROWS), :]
+        copy = pltpu.make_async_remote_copy(
+            src_ref=outgoing.at[away],
+            dst_ref=incoming.at[away],
+            send_sem=image_send.at[away],
+            recv_sem=image_recv.at[away],
+            device_id={"shot": owner},
+            device_id_type=MESH,
+        )
+        copy.start()
+        image_copies.append(copy)
+    strip = placed[:, pl.ds(AX - a + me * ROWS, ROWS), :]
+    kept = jnp.where(lane >= b, strip, 0.0)
+    left, right = kept, strip - kept
+    for away in range(1, SHOTS):
+        offset_copies[away - 1].wait_recv()
+        image_copies[away - 1].wait_recv()
+        sender = (me + SHOTS - away) % SHOTS
+        strip = incoming[away]
+        kept = jnp.where(lane >= offsets[sender, 0:1, :], strip, 0.0)
+        left, right = left + kept, right + (strip - kept)
+    out_ref[:, :, 0:AY] = left
+    out_ref[:, :, AY:GY] = right[:, :, 0:TAIL]
+
+    for copy in model_copies + offset_copies + image_copies + list(halos.values()):
+        copy.wait_send()
+
+
+def fused_shards(
+    forward_field,
+    forward_older,
+    adjoint_field,
+    adjoint_newer,
+    velocity,
+    anchor_first,
+    anchor_second,
+    wavelet,
+    source_cell,
+    receivers,
+    traces,
+):
+    scalars = pl.BlockSpec(memory_space=pltpu.SMEM)
+    vectors = pl.BlockSpec(memory_space=pltpu.VMEM)
+    return pl.pallas_call(
+        window_kernel,
+        out_shape=jax.ShapeDtypeStruct((SLAB, ROWS, GY), jnp.float32),
+        in_specs=[scalars] * 4 + [vectors] * 7,
+        out_specs=vectors,
+        scratch_shapes=[
+            pltpu.VMEM((2, STEPS + 2, SLAB + 2 * REACH, AX + 2 * PAD, AY), jnp.float32),
+            pltpu.VMEM((SLAB + SLAB // 2, GX, AY), jnp.float32),
+            pltpu.VMEM((SLAB, AX, AY), jnp.float32),
+            pltpu.VMEM((STEPS, SLAB, AX, AY), jnp.float32),
+            pltpu.VMEM((SLAB, AX + GX, AY), jnp.float32),
+            pltpu.VMEM((SHOTS, SLAB, ROWS, AY), jnp.float32),
+            pltpu.VMEM((SHOTS, SLAB, ROWS, AY), jnp.float32),
+            pltpu.VMEM((SHOTS, 8, AY), jnp.int32),
+            pltpu.VMEM((8, AY), jnp.int32),
+            pltpu.SemaphoreType.DMA((2, STEPS)),
+            pltpu.SemaphoreType.DMA((2, STEPS)),
+            pltpu.SemaphoreType.DMA((2 * LEVELS - 1,)),
+            pltpu.SemaphoreType.DMA((SHOTS,)),
+            pltpu.SemaphoreType.DMA((SHOTS,)),
+            pltpu.SemaphoreType.DMA((SHOTS,)),
+            pltpu.SemaphoreType.DMA((SHOTS,)),
+            pltpu.SemaphoreType.DMA((SHOTS,)),
+        ],
+        compiler_params=pltpu.CompilerParams(
+            collective_id=0, has_side_effects=True, vmem_limit_bytes=40 << 20
+        ),
+    )(
+        anchor_first,
+        anchor_second,
+        wavelet,
+        source_cell,
+        receivers,
+        traces,
+        forward_field,
+        forward_older,
+        adjoint_field,
+        adjoint_newer,
+        velocity,
+    )
+
+
+def fits_kernel(mesh):
+    return mesh.shape["shot"] == SHOTS and mesh.shape["ap"] == 2
+
+
 def solution(mesh):
+    body = fused_shards if fits_kernel(mesh) else shards
     in_specs = (
         P(("groups", "shot"), "ap", None, None),
         P(("groups", "shot"), "ap", None, None),
@@ -161,4 +499,4 @@
         P(("groups", "shot"), None, None),
     )
     out_specs = P(("groups", "ap"), "shot", None)
-    return jax.shard_map(shards, mesh=mesh, in_specs=in_specs, out_specs=out_specs, check_vma=False)
+    return jax.shard_map(body, mesh=mesh, in_specs=in_specs, out_specs=out_specs, check_vma=False)

time: 201 us -> 50.3 us (0.25)
  waiting for transfers between devices: 63.9 us -> 0 us
  Pallas kernels: 0 us -> 42.9 us
  other arithmetic: 35.9 us -> 0 us
  blocking collectives: 35.7 us -> 0 us
  starting transfers between devices: 35.7 us -> 0 us
  between operations: 16.5 us -> 2.04 us
  local copies, waits for them, and re-layouts: 13.1 us -> 5.18 us
    reduce_scatter x1 -> x0, waiting for transfers between devices: 63.4 us -> none  [shards(): lax.psum_scatter(partial_image, 'shot', scatter_dimension=1, tiled=True)]
    pallas_call x0 -> x1, Pallas kernels: none -> 42.9 us  [fused_shards(): pl.pallas_call(window_kernel, out_shape=jax.ShapeDtypeStruct((SLAB, ROWS,...]
    all_gather x1 -> x0, blocking collectives: 35.7 us -> none  [shards(): speed_model = lax.all_gather(velocity, 'shot', axis=1, tiled=True)]
    ppermute x16 -> x0, starting transfers between devices: 35.7 us -> none  [the longest x8 25.2 us: with_halo(): before = lax.ppermute(last, axis, up)]
    scatter-add x8 -> x0, other arithmetic: 16.4 us -> none  [inject(): flat = jnp.zeros((row_count * plane,), jnp.float32).at[jnp.where(inside,...]
    add x6 -> x0, other arithmetic: 10.2 us -> none  [advance(): 2.0 * current - previous]
    div x1 -> x0, other arithmetic: 5.29 us -> none  [shards(): shot_image = correlation / STEPS]
    slice x10 -> x0, local copies, waits for them, and re-layouts: 4.83 us -> none  [the longest x6 3.3 us: with_halo(): initial = lax.slice_in_dim(shard, 0, width, axis=dim)]
  transfers between devices with their start and end apart: 17 -> 0, of which waited for: 2 -> 0; matrix products, arithmetic and copies ran while one was open for 17% -> 0% of each run, Pallas kernels for 0% -> 0%
where the time goes in v1:
time: 50.3 us; the launch traced here: 50.1 us
  Pallas kernels  42.9 us (85%)
  local copies, waits for them, and re-layouts  5.18 us (10%)
  between operations  2.04 us (4%)
    pallas_call x1, Pallas kernels, fused_shards(): pl.pallas_call(window_kernel, out_shape=jax.ShapeDtypeStruct((SLAB, ROWS,...  42.9 us
    unnamed x17, local copies, waits for them, and re-layouts  5.18 us

profile of v1, /device:TPU:0, one launch (start us, length us, event | category | flops | bytes accessed | tf_op | source)
XLA Modules:
  0.0 50.1 jit_solution(12533763159918104026)
XLA Ops:
  0.0 0.0 copy-start.5
  1.3 0.0 copy-start.6
  1.3 0.0 copy-start.7
  2.0 0.0 copy-done.5
  2.0 0.0 copy-done.6
  2.0 0.0 copy-done.7
  2.0 0.0 copy-start
  2.0 0.9 %copy-done = bf16[1,8,64,128]{3,2,1,0:T(8,128)(2,1)S(1)} copy-done((bf16[1,8,64,128]{3,2,1,0:T(8,128)(2,1)S(1)}, bf16[1,8,64,128]{3,2,1,0:T(8,128)(2,1)}, u32[]{:S(2)}) %copy-start) | copy-done | bytes 131096
  2.9 0.0 copy-start.1
  2.9 0.9 %copy-done.1 = bf16[1,8,64,128]{3,2,1,0:T(8,128)(2,1)S(1)} copy-done((bf16[1,8,64,128]{3,2,1,0:T(8,128)(2,1)S(1)}, bf16[1,8,64,128]{3,2,1,0:T(8,128)(2,1)}, u32[]{:S(2)}) %copy-start.1) | copy-done | bytes 131096
  3.8 0.0 copy-start.2
  3.8 0.9 %copy-done.2 = bf16[1,8,64,128]{3,2,1,0:T(8,128)(2,1)S(1)} copy-done((bf16[1,8,64,128]{3,2,1,0:T(8,128)(2,1)S(1)}, bf16[1,8,64,128]{3,2,1,0:T(8,128)(2,1)}, u32[]{:S(2)}) %copy-start.2) | copy-done | bytes 131096
  4.7 0.0 copy-start.3
  4.7 0.9 %copy-done.3 = bf16[1,8,64,128]{3,2,1,0:T(8,128)(2,1)S(1)} copy-done((bf16[1,8,64,128]{3,2,1,0:T(8,128)(2,1)S(1)}, bf16[1,8,64,128]{3,2,1,0:T(8,128)(2,1)}, u32[]{:S(2)}) %copy-start.3) | copy-done | bytes 131096
  5.6 0.0 copy-start.4
  5.6 0.9 %copy-done.4 = f32[8,16,192]{2,1,0:T(8,128)S(1)} copy-done((f32[8,16,192]{2,1,0:T(8,128)S(1)}, f32[8,16,192]{2,1,0:T(8,128)}, u32[]{:S(2)}) %copy-start.4) | copy-done | bytes 98328
  6.6 42.9 %shard_map.109 = f32[8,16,192]{2,1,0:T(8,128)S(1)} custom-call(s32[1]{0:T(128)S(6)} %copy.13.a_ref, s32[1]{0:T(128)S(6)} %copy.14.b_ref, f32[1,4]{1,0:T(1,128)S(1)} %copy-done.7, s32[1]{0:T(128)S(6)} %copy.15.source_ref, s32[1,256]{1,0:T(1,128)S(1)} %copy-done.6, f32[1,4,256]{2,1,0:T(4,128)S(1)} %copy-done.5, bf16[1,8,64,128]{3,2,1,0:T(8,128)(2,1)S(1)} %copy-done, ...), custom_call_target="tpu_custom_call" | custom-call | tf_op jit(solution)/shard_map/pallas_call | solution.py:440
  49.4 0.7 %copy.16 = f32[8,16,192]{2,1,0:T(8,128)} copy(f32[8,16,192]{2,1,0:T(8,128)S(1)} %shard_map.109) | data formatting | bytes 196608
Async XLA Ops:
  0.0 2.0 %copy-start.5 = (f32[1,4,256]{2,1,0:T(4,128)S(1)}, f32[1,4,256]{2,1,0:T(4,128)}, u32[]{:S(2)}) copy-start(f32[1,4,256]{2,1,0:T(4,128)} %traces_ref.1) | copy-start | bytes 12292
  1.3 0.7 %copy-start.6 = (s32[1,256]{1,0:T(1,128)S(1)}, s32[1,256]{1,0:T(1,128)}, u32[]{:S(2)}) copy-start(s32[1,256]{1,0:T(1,128)} %receivers_ref.1) | copy-start | bytes 3076
  1.3 0.7 %copy-start.7 = (f32[1,4]{1,0:T(1,128)S(1)}, f32[1,4]{1,0:T(1,128)}, u32[]{:S(2)}) copy-start(f32[1,4]{1,0:T(1,128)} %wavelet_ref.1) | copy-start | bytes 52
  2.0 0.9 %copy-start = (bf16[1,8,64,128]{3,2,1,0:T(8,128)(2,1)S(1)}, bf16[1,8,64,128]{3,2,1,0:T(8,128)(2,1)}, u32[]{:S(2)}) copy-start(bf16[1,8,64,128]{3,2,1,0:T(8,128)(2,1)} %forward_ref.1) | copy-start | bytes 393220
  2.9 0.9 %copy-start.1 = (bf16[1,8,64,128]{3,2,1,0:T(8,128)(2,1)S(1)}, bf16[1,8,64,128]{3,2,1,0:T(8,128)(2,1)}, u32[]{:S(2)}) copy-start(bf16[1,8,64,128]{3,2,1,0:T(8,128)(2,1)} %forward_older_ref.1) | copy-start | bytes 393220
  3.8 0.9 %copy-start.2 = (bf16[1,8,64,128]{3,2,1,0:T(8,128)(2,1)S(1)}, bf16[1,8,64,128]{3,2,1,0:T(8,128)(2,1)}, u32[]{:S(2)}) copy-start(bf16[1,8,64,128]{3,2,1,0:T(8,128)(2,1)} %adjoint_ref.1) | copy-start | bytes 393220
  4.7 0.9 %copy-start.3 = (bf16[1,8,64,128]{3,2,1,0:T(8,128)(2,1)S(1)}, bf16[1,8,64,128]{3,2,1,0:T(8,128)(2,1)}, u32[]{:S(2)}) copy-start(bf16[1,8,64,128]{3,2,1,0:T(8,128)(2,1)} %adjoint_newer_ref.1) | copy-start | bytes 393220
  5.6 0.9 %copy-start.4 = (f32[8,16,192]{2,1,0:T(8,128)S(1)}, f32[8,16,192]{2,1,0:T(8,128)}, u32[]{:S(2)}) copy-start(f32[8,16,192]{2,1,0:T(8,128)} %velocity_ref.1) | copy-start | bytes 294916

commit v2 on v1

--- a/solution.py
+++ b/solution.py
@@ -155,10 +155,23 @@
 TAIL = GY - AY
 PAD = 8
 REACH = 4
+UNROLL = 4
 MESH = pl.DeviceIdType.MESH
 
 
 def window_kernel(
+    a_hbm,
+    b_hbm,
+    wavelet_hbm,
+    source_hbm,
+    receivers_hbm,
+    traces_hbm,
+    forward_hbm,
+    forward_older_hbm,
+    adjoint_hbm,
+    adjoint_newer_hbm,
+    velocity_hbm,
+    out_ref,
     a_ref,
     b_ref,
     wavelet_ref,
@@ -170,7 +183,7 @@
     adjoint_ref,
     adjoint_newer_ref,
     velocity_ref,
-    out_ref,
+    load_sem,
     state,
     model,
     coefficient,
@@ -200,9 +213,45 @@
             barrier, inc=1, device_id={"shot": (me + away) % SHOTS}, device_id_type=MESH
         )
 
-    a = a_ref[0]
-    b = b_ref[0]
+    loads = []
+    for source, target in (
+        (velocity_hbm, velocity_ref),
+        (b_hbm, b_ref),
+        (forward_hbm, forward_ref),
+        (adjoint_hbm, adjoint_ref),
+        (receivers_hbm, receivers_ref),
+        (traces_hbm, traces_ref),
+        (forward_older_hbm, forward_older_ref),
+        (adjoint_newer_hbm, adjoint_newer_ref),
+        (a_hbm, a_ref),
+        (wavelet_hbm, wavelet_ref),
+        (source_hbm, source_ref),
+    ):
+        load = pltpu.make_async_copy(source, target, load_sem.at[len(loads)])
+        load.start()
+        loads.append(load)
+
     lane = lax.broadcasted_iota(jnp.int32, (1, AY), 1)
+
+    outer = pl.ds((REACH + SLAB) * half, REACH)
+    inner = pl.ds(PAD, AX)
+    for f in range(2):
+        for k in range(1, STEPS + 1):
+
+            def clear(z, carry):
+                state[f, k, z + REACH, 0:PAD, :] = jnp.zeros((PAD, AY), jnp.float32)
+                state[f, k, z + REACH, PAD + AX :, :] = jnp.zeros((PAD, AY), jnp.float32)
+                return carry
+
+            lax.fori_loop(0, SLAB, clear, 0)
+            state[f, k, outer, inner, :] = jnp.zeros((REACH, AX, AY), jnp.float32)
+
+    def blank(z, carry):
+        placed[z, 0:AX, :] = jnp.zeros((AX, AY), jnp.float32)
+        placed[z, 2 * AX :, :] = jnp.zeros((GX - AX, AY), jnp.float32)
+        return carry
+
+    loads[0].wait()
 
     mine = pl.ds(pl.multiple_of(me * ROWS, ROWS), ROWS)
     for z in range(SLAB):
@@ -211,6 +260,8 @@
         model[SLAB + z, mine, :] = jnp.concatenate(
             [velocity_ref[z, :, AY:GY], velocity_ref[z + SLAB // 2, :, AY:GY]], axis=1
         )
+    loads[1].wait()
+    b = b_ref[0]
     offset_tile[...] = jnp.full((8, AY), b, jnp.int32)
 
     pl.semaphore_wait(barrier, SHOTS)
@@ -227,14 +278,32 @@
         )
 
     across = level * COLUMNS + 1 - column
-    model_copies = []
-    for away in range(1, LEVELS):
-        copy = model_copy(me, away, (level + away) % LEVELS * COLUMNS + column)
-        copy.start()
-        model_copies.append(copy)
-    copy = model_copy(me, 0, across)
-    copy.start()
-    model_copies.append(copy)
+    sends = []
+
+    def send(block, slot, target, needed):
+        copy = model_copy(block, slot, target)
+        pl.when(needed)(copy.start)
+        sends.append((copy, needed))
+
+    for slot, side in enumerate((1, -1)):
+        beside = level + side
+        inside = jnp.logical_and(beside >= 0, beside < LEVELS)
+        send(me, slot, jnp.clip(beside, 0, LEVELS - 1) * COLUMNS + column, inside)
+    send(me, 2, across, level >= 0)
+
+    def pass_on(distance):
+        for side in range(2):
+            step = 1 - 2 * side
+            origin = level - step * distance
+            there = jnp.logical_and(origin >= 0, origin < LEVELS)
+            beside = level + step
+            onward = jnp.logical_and(there, jnp.logical_and(beside >= 0, beside < LEVELS))
+            block = jnp.clip(origin, 0, LEVELS - 1) * COLUMNS + column
+            pl.when(there)(model_copy(block, 0, across).wait_recv)
+            slot = 3 + 4 * (distance - 1) + 2 * side
+            if distance + 1 < LEVELS:
+                send(block, slot, jnp.clip(beside, 0, LEVELS - 1) * COLUMNS + column, onward)
+            send(block, slot + 1, across, there)
 
     offset_copies = []
     for away in range(1, SHOTS):
@@ -250,28 +319,6 @@
         offset_copies.append(copy)
     offsets[me] = offset_tile[...]
 
-    outer = pl.ds((REACH + SLAB) * (half), REACH)
-    inner = pl.ds(PAD, AX)
-    for f, (older, now) in enumerate(
-        ((forward_older_ref, forward_ref), (adjoint_newer_ref, adjoint_ref))
-    ):
-        for k in range(1, STEPS + 1):
-
-            def clear(z, carry):
-                state[f, k, z + REACH, 0:PAD, :] = jnp.zeros((PAD, AY), jnp.float32)
-                state[f, k, z + REACH, PAD + AX :, :] = jnp.zeros((PAD, AY), jnp.float32)
-                return carry
-
-            lax.fori_loop(0, SLAB, clear, 0)
-            state[f, k, outer, inner, :] = jnp.zeros((REACH, AX, AY), jnp.float32)
-
-        def load(z, carry):
-            state[f, 0, z + REACH, inner, :] = older[0, z].astype(jnp.float32)
-            state[f, 1, z + REACH, inner, :] = now[0, z].astype(jnp.float32)
-            return carry
-
-        lax.fori_loop(0, SLAB, load, 0)
-
     def halo_copy(f, k):
         return pltpu.make_async_remote_copy(
             src_ref=state.at[f, k, pl.ds(2 * REACH - REACH * half, REACH), inner, :],
@@ -283,10 +330,28 @@
         )
 
     halos = {}
-    for f in range(2):
+    for f, now in enumerate((forward_ref, adjoint_ref)):
+        loads[2 + f].wait()
+
+        def widen(z, carry):
+            state[f, 1, z + REACH, inner, :] = now[0, z].astype(jnp.float32)
+            return carry
+
+        lax.fori_loop(0, SLAB, widen, 0)
         halos[f, 1] = halo_copy(f, 1)
         halos[f, 1].start()
-
+    lax.fori_loop(0, SLAB, blank, 0)
+    for f, older in enumerate((forward_older_ref, adjoint_newer_ref)):
+        loads[6 + f].wait()
+
+        def widen(z, carry):
+            state[f, 0, z + REACH, inner, :] = older[0, z].astype(jnp.float32)
+            return carry
+
+        lax.fori_loop(0, SLAB, widen, 0)
+
+    loads[4].wait()
+    loads[5].wait()
     cells = receivers_ref[...]
     count = cells.shape[1]
     row_of = cells // AY - half * (SLAB * AX)
@@ -307,36 +372,9 @@
         )
         injected[k] = (both[:, :AY] + both[:, AY:]).reshape(SLAB, AX, AY)
 
-    def blank(z, carry):
-        placed[z, 0:AX, :] = jnp.zeros((AX, AY), jnp.float32)
-        placed[z, 2 * AX :, :] = jnp.zeros((GX - AX, AY), jnp.float32)
-        return carry
-
-    lax.fori_loop(0, SLAB, blank, 0)
-
-    for away in range(1, LEVELS):
-        block = (level + LEVELS - away) % LEVELS * COLUMNS + column
-        model_copy(block, 0, across).wait_recv()
-        copy = model_copy(block, LEVELS - 1 + away, across)
-        copy.start()
-        model_copies.append(copy)
-    for away in range(LEVELS):
-        block = (level + LEVELS - away) % LEVELS * COLUMNS + 1 - column
-        model_copy(block, 0, across).wait_recv()
-
-    def square(z, carry):
-        rows = pl.ds(a, AX)
-        for part in range(2):
-            tail = model[SLAB + z, rows, :]
-            if part:
-                tail = pltpu.roll(tail, TAIL, 1)
-            joined = jnp.where(lane >= b, model[z + part * (SLAB // 2), rows, :], tail)
-            window = pltpu.roll(joined, (AY - b) % AY, 1)
-            coefficient[z + part * (SLAB // 2)] = window * window
-        return carry
-
-    lax.fori_loop(0, SLAB // 2, square, 0)
-
+    for load in loads[8:]:
+        load.wait()
+    a = a_ref[0]
     flat = (
         lax.broadcasted_iota(jnp.int32, (AX, AY), 0) * AY
         + lax.broadcasted_iota(jnp.int32, (AX, AY), 1)
@@ -363,15 +401,55 @@
                 total = total + jnp.where(flat == here, wavelet_ref[0, k], 0.0)
             else:
                 total = total + injected[k, z]
-            state[f, k + 2, slot, inner, :] = (
-                2.0 * centre - state[f, k, slot, inner, :] + coefficient[z] * total
+            if k > 0:
+                total = 2.0 * centre - state[f, k, slot, inner, :] + coefficient[z] * total
+            state[f, k + 2, slot, inner, :] = total
+            return carry
+
+        lax.fori_loop(0, REACH if k > 0 else SLAB, layer, 0, unroll=UNROLL)
+
+    pass_on(1)
+    for f in range(2):
+        halos[f, 1].wait_recv()
+        layers(f, 0, 0)
+        pass_on(2 + f)
+    for away in range(LEVELS):
+        block = (level + LEVELS - away) % LEVELS * COLUMNS + 1 - column
+        model_copy(block, 0, across).wait_recv()
+
+    def square(z, carry):
+        rows = pl.ds(a, AX)
+        for part in range(2):
+            tail = model[SLAB + z, rows, :]
+            if part:
+                tail = pltpu.roll(tail, TAIL, 1)
+            joined = jnp.where(lane >= b, model[z + part * (SLAB // 2), rows, :], tail)
+            window = pltpu.roll(joined, (AY - b) % AY, 1)
+            coefficient[z + part * (SLAB // 2)] = window * window
+        return carry
+
+    lax.fori_loop(0, SLAB // 2, square, 0)
+
+    def first_step(f, first):
+        def layer(i, carry):
+            slot = first + i + REACH
+            state[f, 2, slot, inner, :] = (
+                2.0 * state[f, 1, slot, inner, :]
+                - state[f, 0, slot, inner, :]
+                + coefficient[first + i] * state[f, 2, slot, inner, :]
             )
             return carry
 
         lax.fori_loop(0, REACH, layer, 0)
 
     far, edge = REACH * half, REACH - REACH * half
-    for k in range(STEPS):
+    for f in range(2):
+        first_step(f, edge)
+        halos[f, 2] = halo_copy(f, 2)
+        halos[f, 2].start()
+    for f in range(2):
+        first_step(f, far)
+    for k in range(1, STEPS):
         layers(0, k, far)
         layers(1, k, far)
         for f in range(2):
@@ -418,7 +496,9 @@
     out_ref[:, :, 0:AY] = left
     out_ref[:, :, AY:GY] = right[:, :, 0:TAIL]
 
-    for copy in model_copies + offset_copies + image_copies + list(halos.values()):
+    for copy, needed in sends:
+        pl.when(needed)(copy.wait_send)
+    for copy in offset_copies + image_copies + list(halos.values()):
         copy.wait_send()
 
 
@@ -435,14 +515,24 @@
     receivers,
     traces,
 ):
-    scalars = pl.BlockSpec(memory_space=pltpu.SMEM)
-    vectors = pl.BlockSpec(memory_space=pltpu.VMEM)
     return pl.pallas_call(
         window_kernel,
         out_shape=jax.ShapeDtypeStruct((SLAB, ROWS, GY), jnp.float32),
-        in_specs=[scalars] * 4 + [vectors] * 7,
-        out_specs=vectors,
+        in_specs=[pl.BlockSpec(memory_space=pl.ANY)] * 11,
+        out_specs=pl.BlockSpec(memory_space=pltpu.VMEM),
         scratch_shapes=[
+            pltpu.SMEM((1,), jnp.int32),
+            pltpu.SMEM((1,), jnp.int32),
+            pltpu.SMEM(wavelet.shape, jnp.float32),
+            pltpu.SMEM((1,), jnp.int32),
+            pltpu.VMEM(receivers.shape, jnp.int32),
+            pltpu.VMEM(traces.shape, jnp.float32),
+            pltpu.VMEM(forward_field.shape, jnp.bfloat16),
+            pltpu.VMEM(forward_field.shape, jnp.bfloat16),
+            pltpu.VMEM(forward_field.shape, jnp.bfloat16),
+            pltpu.VMEM(forward_field.shape, jnp.bfloat16),
+            pltpu.VMEM(velocity.shape, jnp.float32),
+            pltpu.SemaphoreType.DMA((11,)),
             pltpu.VMEM((2, STEPS + 2, SLAB + 2 * REACH, AX + 2 * PAD, AY), jnp.float32),
             pltpu.VMEM((SLAB + SLAB // 2, GX, AY), jnp.float32),
             pltpu.VMEM((SLAB, AX, AY), jnp.float32),
@@ -454,7 +544,7 @@
             pltpu.VMEM((8, AY), jnp.int32),
             pltpu.SemaphoreType.DMA((2, STEPS)),
             pltpu.SemaphoreType.DMA((2, STEPS)),
-            pltpu.SemaphoreType.DMA((2 * LEVELS - 1,)),
+            pltpu.SemaphoreType.DMA((3 + 4 * (LEVELS - 1),)),
             pltpu.SemaphoreType.DMA((SHOTS,)),
             pltpu.SemaphoreType.DMA((SHOTS,)),
             pltpu.SemaphoreType.DMA((SHOTS,)),
@@ -462,7 +552,7 @@
             pltpu.SemaphoreType.DMA((SHOTS,)),
         ],
         compiler_params=pltpu.CompilerParams(
-            collective_id=0, has_side_effects=True, vmem_limit_bytes=40 << 20
+            collective_id=0, has_side_effects=True, vmem_limit_bytes=63 << 20
         ),
     )(
         anchor_first,

time: 50.3 us -> 40.2 us (0.80)
  Pallas kernels: 42.9 us -> 36.5 us
  local copies, waits for them, and re-layouts: 5.18 us -> 1.57 us
    pallas_call x1, Pallas kernels: 42.9 us -> 36.5 us  [fused_shards(): pl.pallas_call(window_kernel, out_shape=jax.ShapeDtypeStruct((SLAB, ROWS,...]
    unnamed x17 -> x1, local copies, waits for them, and re-layouts: 5.18 us -> 1.57 us
where the time goes in v2:
time: 40.2 us; the launch traced here: 40 us
  Pallas kernels  36.5 us (91%)
  between operations  1.95 us (5%)
  local copies, waits for them, and re-layouts  1.57 us (4%)
    pallas_call x1, Pallas kernels, fused_shards(): pl.pallas_call(window_kernel, out_shape=jax.ShapeDtypeStruct((SLAB, ROWS,...  36.5 us
    unnamed x1, local copies, waits for them, and re-layouts  1.57 us

profile of v2, /device:TPU:0, one launch (start us, length us, event | category | flops | bytes accessed | tf_op | source)
XLA Modules:
  0.0 40.0 jit_solution(8560310118474106941)
XLA Ops:
  1.9 36.5 %shard_map.109 = f32[8,16,192]{2,1,0:T(8,128)} custom-call(s32[1]{0:T(128)S(6)} %copy.13.a_hbm, s32[1]{0:T(128)S(6)} %copy.14.b_hbm, f32[1,4]{1,0:T(1,128)} %wavelet_hbm.1, s32[1]{0:T(128)S(6)} %copy.15.source_hbm, s32[1,256]{1,0:T(1,128)} %receivers_hbm.1, f32[1,4,256]{2,1,0:T(4,128)} %traces_hbm.1, bf16[1,8,64,128]{3,2,1,0:T(8,128)(2,1)} %forward_hbm.1, ...), custom_call_target="tpu_custom_call" | custom-call | tf_op jit(solution)/shard_map/pallas_call | solution.py:518
  38.4 1.6 %copy.16 = f32[8,16,192]{2,1,0:T(8,128)} copy(f32[8,16,192]{2,1,0:T(8,128)} %shard_map.109) | data formatting | bytes 196608

commit v3 on v2

--- a/solution.py
+++ b/solution.py
@@ -449,16 +449,6 @@
         halos[f, 2].start()
     for f in range(2):
         first_step(f, far)
-    for k in range(1, STEPS):
-        layers(0, k, far)
-        layers(1, k, far)
-        for f in range(2):
-            halos[f, k + 1].wait_recv()
-            layers(f, k, edge)
-            if k + 1 < STEPS:
-                halos[f, k + 2] = halo_copy(f, k + 2)
-                halos[f, k + 2].start()
-
     def correlate(z, carry):
         slot = z + REACH
         image = state[0, 2, slot, inner, :] * state[1, STEPS + 1, slot, inner, :]
@@ -467,28 +457,45 @@
         placed[z, pl.ds(AX, AX), :] = pltpu.roll(image * (1.0 / STEPS), b, 1)
         return carry
 
-    lax.fori_loop(0, SLAB, correlate, 0)
-
     image_copies = []
-    for away in range(1, SHOTS):
-        owner = (me + away) % SHOTS
-        outgoing[away] = placed[:, pl.ds(AX - a + owner * ROWS, ROWS), :]
-        copy = pltpu.make_async_remote_copy(
-            src_ref=outgoing.at[away],
-            dst_ref=incoming.at[away],
-            send_sem=image_send.at[away],
-            recv_sem=image_recv.at[away],
-            device_id={"shot": owner},
-            device_id_type=MESH,
-        )
-        copy.start()
-        image_copies.append(copy)
+
+    def deliver(part, first):
+        lax.fori_loop(first, first + REACH, correlate, 0)
+        some = pl.ds(first, REACH)
+        for away in range(1, SHOTS):
+            owner = (me + away) % SHOTS
+            outgoing[away, some] = placed[some, pl.ds(AX - a + owner * ROWS, ROWS), :]
+            copy = pltpu.make_async_remote_copy(
+                src_ref=outgoing.at[away, some],
+                dst_ref=incoming.at[away, some],
+                send_sem=image_send.at[part * SHOTS + away],
+                recv_sem=image_recv.at[part * SHOTS + away],
+                device_id={"shot": owner},
+                device_id_type=MESH,
+            )
+            copy.start()
+            image_copies.append(copy)
+
+    for k in range(1, STEPS):
+        layers(0, k, far)
+        layers(1, k, far)
+        if k + 1 == STEPS:
+            deliver(0, far)
+        for f in range(2):
+            halos[f, k + 1].wait_recv()
+            layers(f, k, edge)
+            if k + 1 < STEPS:
+                halos[f, k + 2] = halo_copy(f, k + 2)
+                halos[f, k + 2].start()
+
+    deliver(1, edge)
     strip = placed[:, pl.ds(AX - a + me * ROWS, ROWS), :]
     kept = jnp.where(lane >= b, strip, 0.0)
     left, right = kept, strip - kept
     for away in range(1, SHOTS):
         offset_copies[away - 1].wait_recv()
         image_copies[away - 1].wait_recv()
+        image_copies[SHOTS + away - 2].wait_recv()
         sender = (me + SHOTS - away) % SHOTS
         strip = incoming[away]
         kept = jnp.where(lane >= offsets[sender, 0:1, :], strip, 0.0)
@@ -546,8 +553,8 @@
             pltpu.SemaphoreType.DMA((2, STEPS)),
             pltpu.SemaphoreType.DMA((3 + 4 * (LEVELS - 1),)),
             pltpu.SemaphoreType.DMA((SHOTS,)),
-            pltpu.SemaphoreType.DMA((SHOTS,)),
-            pltpu.SemaphoreType.DMA((SHOTS,)),
+            pltpu.SemaphoreType.DMA((2 * SHOTS,)),
+            pltpu.SemaphoreType.DMA((2 * SHOTS,)),
             pltpu.SemaphoreType.DMA((SHOTS,)),
             pltpu.SemaphoreType.DMA((SHOTS,)),
         ],

time: 40.2 us -> 39.9 us (level)
  no operation moved by 1% of the time
where the time goes in v3:
time: 39.9 us; the launch traced here: 39.7 us
  Pallas kernels  36.2 us (91%)
  between operations  1.95 us (5%)
  local copies, waits for them, and re-layouts  1.57 us (4%)
    pallas_call x1, Pallas kernels, fused_shards(): pl.pallas_call(window_kernel, out_shape=jax.ShapeDtypeStruct((SLAB, ROWS,...  36.2 us
    unnamed x1, local copies, waits for them, and re-layouts  1.57 us

profile of v3, /device:TPU:0, one launch (start us, length us, event | category | flops | bytes accessed | tf_op | source)
XLA Modules:
  0.0 39.7 jit_solution(5702038662117689227)
XLA Ops:
  1.9 36.2 %shard_map.109 = f32[8,16,192]{2,1,0:T(8,128)} custom-call(s32[1]{0:T(128)S(6)} %copy.13.a_hbm, s32[1]{0:T(128)S(6)} %copy.14.b_hbm, f32[1,4]{1,0:T(1,128)} %wavelet_hbm.1, s32[1]{0:T(128)S(6)} %copy.15.source_hbm, s32[1,256]{1,0:T(1,128)} %receivers_hbm.1, f32[1,4,256]{2,1,0:T(4,128)} %traces_hbm.1, bf16[1,8,64,128]{3,2,1,0:T(8,128)(2,1)} %forward_hbm.1, ...), custom_call_target="tpu_custom_call" | custom-call | tf_op jit(solution)/shard_map/pallas_call | solution.py:525
  38.2 1.6 %copy.16 = f32[8,16,192]{2,1,0:T(8,128)} copy(f32[8,16,192]{2,1,0:T(8,128)} %shard_map.109) | data formatting | bytes 196608
